TPU v7x, 256 devices: a whole 4x4x8 slice. The times are simulated.
256 devices in a mesh: seq: 64 (over x_lo, z, y), head: 4 (over x_hi, core).
Axes of the slice: x: 4 (x_hi: 2, x_lo: 2; x = x_hi * 2 + x_lo), y: 4, z: 8, core: 2. Of those that a mesh axis runs over, the one named last changes fastest.
Arguments:
- level_input: bfloat16 [32768, 1536], P('seq', 'head'), may hold values from -6 to 6
- norm_gain: float32 [1536], replicated, may hold values from 0.1 to 1.9
- query_weight: bfloat16 [1536, 1024], P(None, 'head'), may hold values from -0.15625 to 0.15625
- key_weight: bfloat16 [1536, 128], replicated, may hold values from -0.15625 to 0.15625
- value_weight: bfloat16 [1536, 192], replicated, may hold values from -0.15625 to 0.15625
- out_weight: bfloat16 [1536, 1536], P('head'), may hold values from -0.15625 to 0.15625
- up_weight: bfloat16 [5, 1536, 1536], P(None, None, 'head'), may hold values from -0.0625 to 0.0625
- grad_output: bfloat16 [32768, 1536], P('seq', 'head'), may hold values from -6 to 6
Outputs:
- level_output: bfloat16 [32768, 1536], P('seq', 'head')
- grad_mixed: bfloat16 [16384, 1536], P('seq', 'head')
All inputs are finite; a program needn't handle non-finite values.
Results may differ from a plain program's by a relative error of at most 0.015.
Values may be sent and summed in bfloat16 or wider, within the bound.
A program may use at most 128 MiB of HBM per device.

v0:
```python
import jax
import jax.numpy as jnp
from jax import lax
from jax.sharding import PartitionSpec as P

DK = 128


score_scale = 24.0
epsilon = 1e-06


def with_halo(block, sides, width):
    for axis, dim in sides:
        count = lax.axis_size(axis)
        forward = [(i, i + 1) for i in range(count - 1)]
        backward = [(target, source) for source, target in forward]
        low = lax.ppermute(
            lax.slice_in_dim(block, block.shape[dim] - width, None, axis=dim), axis, forward
        )
        high = lax.ppermute(lax.slice_in_dim(block, 0, width, axis=dim), axis, backward)
        block = jnp.concatenate([low, block, high], axis=dim)
    return block


def rms_normalize(values):
    return values * lax.rsqrt(jnp.mean(values * values, axis=-1, keepdims=True) + epsilon)


def contract_last(left, right):
    return lax.dot_general(
        left, right, (((1,), (1,)), ((), ())), preferred_element_type=jnp.float32
    )


def project_shared(normed, key_weight, value_weight):
    key_local = rms_normalize(
        jnp.dot(normed, key_weight, preferred_element_type=jnp.float32)
    ).astype(jnp.bfloat16)
    value_local = jnp.dot(normed, value_weight, preferred_element_type=jnp.float32).astype(
        jnp.bfloat16
    )
    return (key_local, value_local)


def make_attend(query_matrix, incoming):
    scores = contract_last(query_matrix, incoming[0]) * (score_scale / DK)
    weights_exp = jnp.exp(scores)
    denominator = jnp.sum(weights_exp, axis=1, keepdims=True)
    numerator = jnp.dot(
        weights_exp.astype(jnp.bfloat16), incoming[1], preferred_element_type=jnp.float32
    )
    return (numerator, denominator)


def per_device(
    level_input,
    norm_gain,
    query_weight,
    key_weight,
    value_weight,
    out_weight,
    up_weight,
    grad_output,
):
    total_rows = level_input.shape[0]
    half_rows = total_rows // 2
    local_heads = query_weight.shape[1] // DK
    value_width = value_weight.shape[1]
    input_float = level_input.astype(jnp.float32)
    pooled = (0.5 * (input_float[0::2] + input_float[1::2])).astype(jnp.bfloat16)
    gathered = lax.all_gather(pooled, "head", axis=1, tiled=True)
    normed = (rms_normalize(gathered.astype(jnp.float32)) * norm_gain).astype(jnp.bfloat16)
    queries = jnp.dot(normed, query_weight, preferred_element_type=jnp.float32)
    queries = rms_normalize(queries.reshape(half_rows, local_heads, DK)).astype(jnp.bfloat16)
    queries_flat = queries.reshape(half_rows * local_heads, DK)
    key_local, value_local = project_shared(normed, key_weight, value_weight)
    numerator, denominator = make_attend(
        queries_flat,
        (
            lax.all_gather(key_local, "seq", axis=0, tiled=True),
            lax.all_gather(value_local, "seq", axis=0, tiled=True),
        ),
    )
    attended = (
        (numerator / denominator).astype(jnp.bfloat16).reshape(half_rows, local_heads * value_width)
    )
    partial_out = jnp.dot(attended, out_weight, preferred_element_type=jnp.float32)
    summed_out = lax.psum_scatter(
        partial_out.astype(jnp.bfloat16), "head", scatter_dimension=1, tiled=True
    ).astype(jnp.float32)
    mixed = (pooled.astype(jnp.float32) + summed_out).astype(jnp.bfloat16)
    rimmed = with_halo(mixed, (("seq", 0),), 1)
    taps = up_weight.shape[0]
    carry = jnp.zeros((total_rows, up_weight.shape[2]), jnp.float32)
    upsampled = jnp.repeat(lax.all_gather(rimmed, "head", axis=1, tiled=True), 2, axis=0)
    for convolve_tap in range(taps):
        tap_rows = up_weight[convolve_tap]
        carry = carry + jnp.dot(
            upsampled[convolve_tap : convolve_tap + total_rows],
            tap_rows,
            preferred_element_type=jnp.float32,
        )
    level_output = (input_float + carry).astype(jnp.bfloat16)
    padded_grad = with_halo(grad_output, (("seq", 0),), 2)
    grad_upsampled = jnp.zeros((total_rows, up_weight.shape[1]), jnp.float32)
    for tap in range(taps):
        grad_upsampled = grad_upsampled + contract_last(
            padded_grad[4 - tap : 4 - tap + total_rows], up_weight[tap]
        )
    paired = grad_upsampled[0::2] + grad_upsampled[1::2]
    grad_mixed = lax.psum_scatter(
        paired.astype(jnp.bfloat16), "head", scatter_dimension=1, tiled=True
    )
    return (level_output, grad_mixed)


def solution(mesh):
    in_specs = (
        P("seq", "head"),
        P(),
        P(None, "head"),
        P(),
        P(),
        P("head", None),
        P(None, None, "head"),
        P("seq", "head"),
    )
    out_specs = (P("seq", "head"), P("seq", "head"))
    return jax.shard_map(
        per_device, mesh=mesh, in_specs=in_specs, out_specs=out_specs, check_vma=False
    )
```

profile of v0, /device:TPU:1, one launch (start us, length us, event | category | flops | bytes accessed | tf_op | source)
XLA Modules:
  0.0 661.9 jit_solution(12378950555142951082)
XLA Ops:
  7.2 2.1 slice.87
  9.4 2.0 slice.88
  11.5 11.9 %all_gather.12 = bf16[256,1536]{1,0:T(8,128)(2,1)S(1)} all-gather(bf16[256,384]{1,0:T(8,128)(2,1)S(1)} %multiply_convert_fusion), channel_id=1, replica_groups=mesh['seq'=64,'head'=4] {'head'}, dimensions={1}, use_global_device_ids=true | all-gather | bytes 983040 | tf_op jit(solution)/shard_map/all_gather | solution.py:72
  27.5 4.0 collective-permute-start.3
  33.2 3.9 fusion.25
  37.6 4.0 fusion.20
  41.7 3.9 fusion.28
  45.6 193.0 %all-gather.3.cloned.1.call-done = bf16[16384,128]{0,1:T(8,128)(2,1)} async-done(((bf16[256,128]{0,1:T(8,128)(2,1)}), bf16[16384,128]{0,1:T(8,128)(2,1)}) %all-gather.3.cloned.1.call-update) | async-done | bytes 4194320 | tf_op jit(solution)/shard_map/all_gather | solution.py:81
  238.6 15.6 %fusion = (f32[512]{0:T(512)S(1)}, f32[512,16384]{1,0:T(8,128)}) fusion(bf16[16384,128]{0,1:T(8,128)(2,1)} %all-gather.3.cloned.1.call-done, f32[512,128]{1,0:T(8,128)S(1)} %reshape.53, f32[512]{0:T(512)S(1)} %rsqrt.29), kind=kOutput, calls=%fused_computation.1 | convolution fusion | flops 2164391424 | bytes 38014976 | tf_op jit(solution)/shard_map/dot_general | solution.py:31
  254.1 237.7 %all-gather.5.cloned.1.call-done = bf16[16384,192]{0,1:T(8,128)(2,1)} async-done(((bf16[256,192]{0,1:T(8,128)(2,1)}), bf16[16384,192]{0,1:T(8,128)(2,1)}) %all-gather.5.cloned.1.call-update) | async-done | bytes 6291472 | tf_op jit(solution)/shard_map/all_gather | solution.py:82
  491.8 15.3 %fusion.37 = bf16[512,192]{0,1:T(8,128)(2,1)S(1)} fusion(bf16[16384,192]{0,1:T(8,128)(2,1)} %all-gather.5.cloned.1.call-done, f32[512,16384]{1,0:T(8,128)} %get-tuple-element.14, f32[512]{0:T(512)S(1)} %get-tuple-element.13), kind=kOutput, calls=%fused_computation.42 | convolution fusion | flops 3238199296 | bytes 40044544 | tf_op jit(solution)/shard_map/dot_general | solution.py:50
  509.4 4.4 fusion.6
  513.8 4.0 fusion.5
  517.8 6.1 slice.110
  523.9 7.1 %slice.111 = f32[256,1536]{1,0:T(8,128)} slice(f32[512,1536]{1,0:T(8,128)} %fusion.5), slice={[1:512:2], [0:1536:1]} | slice | bytes 3145728 | tf_op jit(solution)/shard_map/slice | solution.py:111
  533.8 44.0 %reduce-scatter.7.cloned.1.call-done = bf16[384,256]{1,0:T(8,128)(2,1)} async-done(((bf16[1536,256]{1,0:T(8,128)(2,1)}), bf16[384,256]{1,0:T(8,128)(2,1)}) %reduce-scatter.7.cloned.1.call-update) | async-done | bytes 196624
  579.0 3.1 collective-permute-start
  583.4 32.1 %reduce-scatter.9.cloned.1.call-done = bf16[384,256]{1,0:T(8,128)(2,1)} async-done(((bf16[1536,256]{1,0:T(8,128)(2,1)}), bf16[384,256]{1,0:T(8,128)(2,1)}) %reduce-scatter.9.cloned.1.call-update) | async-done | bytes 196624
  617.3 10.4 %all_gather.15 = bf16[258,1536]{1,0:T(8,128)(2,1)S(1)} all-gather(bf16[258,384]{1,0:T(8,128)(2,1)S(1)} %pad_maximum_fusion.2), channel_id=1, replica_groups=mesh['seq'=64,'head'=4] {'head'}, dimensions={1}, use_global_device_ids=true | all-gather | bytes 990720 | tf_op jit(solution)/shard_map/all_gather | solution.py:96
  631.3 3.6 fusion.32
  637.5 3.8 fusion.10
  641.3 3.2 fusion.14
  649.2 3.1 fusion.17
  652.3 3.0 fusion.19
  (76 shorter events, 26.4 us)
Async XLA Ops:
  7.2 500.3 %copy-start = (bf16[384,1536]{1,0:T(8,128)(2,1)S(1)}, bf16[384,1536]{1,0:T(8,128)(2,1)}, u32[]{:S(2)}) copy-start(bf16[384,1536]{1,0:T(8,128)(2,1)} %param.13) | copy-start | bytes 3538948
  7.2 231.4 %all-gather.3.cloned.1.call-start = ((), (), s32[]{:S(2)}) async-start(), calls=%async_computation.2 | async-start | bytes 4259840 | tf_op jit(solution)/shard_map/all_gather | solution.py:81
  11.4 12.3 %copy-start.10 = (bf16[1536,128]{1,0:T(8,128)(2,1)S(1)}, bf16[1536,128]{1,0:T(8,128)(2,1)}, u32[]{:S(2)}) copy-start(bf16[1536,128]{1,0:T(8,128)(2,1)} %param.11) | copy-start | bytes 1179652
  11.4 12.3 %copy-start.11 = (f32[1536]{0:T(1024)S(1)}, f32[1536]{0:T(1024)}, u32[]{:S(2)}) copy-start(f32[1536]{0:T(1024)} %param.9) | copy-start | bytes 18436
  23.4 1.5 copy-start.9
  24.2 2.0 copy-start.3
  24.9 466.9 %all-gather.5.cloned.1.call-start = ((), (), s32[]{:S(2)}) async-start(), calls=%async_computation.3 | async-start | bytes 6389760 | tf_op jit(solution)/shard_map/all_gather | solution.py:82
  26.1 551.8 %reduce-scatter.7.cloned.1.call-start = ((), (), s32[]{:S(2)}) async-start(), calls=%async_computation.4 | async-start | bytes 983040
  26.2 11.4 %collective-permute-start.2 = (bf16[2,384]{1,0:T(2,128)(2,1)S(1)}, bf16[2,384]{1,0:T(2,128)(2,1)S(1)}, u32[]{:S(2)}, u32[]{:S(2)}) collective-permute-start(bf16[2,384]{1,0:T(2,128)(2,1)S(1)} %get-tuple-element.5), channel_id=1, source_target_pairs={{4,0},{8,4},{12,8},{16,12},{20,16},{24,20},{28,24},{32,28},{36,32}... | collective-permute-start | bytes 4616 | tf_op jit(solution)/shard_map/ppermute | solution.py:21
  27.5 10.1 %collective-permute-start.3 = (bf16[2,384]{1,0:T(2,128)(2,1)S(1)}, bf16[2,384]{1,0:T(2,128)(2,1)S(1)}, u32[]{:S(2)}, u32[]{:S(2)}) collective-permute-start(bf16[2,384]{1,0:T(2,128)(2,1)S(1)} %get-tuple-element.6), channel_id=1, source_target_pairs={{0,4},{4,8},{8,12},{12,16},{16,20},{20,24},{24,28},{28,32},{32,36}... | collective-permute-start | bytes 4616 | tf_op jit(solution)/shard_map/ppermute | solution.py:18
  509.2 106.3 %reduce-scatter.9.cloned.1.call-start = ((), (), s32[]{:S(2)}) async-start(), calls=%async_computation.5 | async-start | bytes 983040
  509.4 4.4 copy-start.2
  579.0 38.3 %collective-permute-start = (bf16[1,384]{1,0:T(2,128)(2,1)S(1)}, bf16[1,384]{1,0:T(2,128)(2,1)S(1)}, u32[]{:S(2)}, u32[]{:S(2)}) collective-permute-start(bf16[1,384]{1,0:T(2,128)(2,1)S(1)} %get-tuple-element.7), channel_id=1, source_target_pairs={{0,4},{4,8},{8,12},{12,16},{16,20},{20,24},{24,28},{28,32},{32,36}... | collective-permute-start | bytes 2312 | tf_op jit(solution)/shard_map/ppermute | solution.py:18
  582.1 35.1 %collective-permute-start.1 = (bf16[1,384]{1,0:T(2,128)(2,1)S(1)}, bf16[1,384]{1,0:T(2,128)(2,1)S(1)}, u32[]{:S(2)}, u32[]{:S(2)}) collective-permute-start(bf16[1,384]{1,0:T(2,128)(2,1)S(1)} %get-tuple-element.8), channel_id=1, source_target_pairs={{4,0},{8,4},{12,8},{16,12},{20,16},{24,20},{28,24},{32,28},{36,32}... | collective-permute-start | bytes 2312 | tf_op jit(solution)/shard_map/ppermute | solution.py:21
  637.5 3.8 copy-start.5
  637.5 3.8 copy-start.12
  641.3 3.2 copy-start.4
  647.7 1.5 copy-start.8
  649.2 3.1 copy-start.6
  649.2 3.1 copy-start.7
  649.2 6.2 copy-start.1
Sparse Core Ops, SparseCore 0:
  25.0 213.5 all-gather.2
  240.9 250.8 all-gather.4
  509.3 68.4 reduce-scatter.6
  580.7 34.7 reduce-scatter.8
where the time goes:
time: 663 us; the launch traced here: 662 us
  waiting for transfers between devices  507 us (76%)
  matrix products  71.7 us (11%)
  local copies, waits for them, and re-layouts  34.3 us (5%)
  blocking collectives  22.3 us (3%)
  between operations  14.1 us (2%)
  starting transfers between devices  10 us (2%)
    all_gather x1, waiting for transfers between devices, per_device(): lax.all_gather(value_local, 'seq', axis=0, tiled=True)  238 us
    all_gather x1, waiting for transfers between devices, per_device(): lax.all_gather(key_local, 'seq', axis=0, tiled=True)  193 us
    unnamed x6, waiting for transfers between devices  76.2 us
    dot_general x6, matrix products, contract_last(): lax.dot_general(left, right, (((1,), (1,)), ((), ())), preferred_element_...  35.8 us
    dot_general x5, matrix products, per_device(): jnp.dot(upsampled[convolve_tap:convolve_tap + total_rows], tap_rows, pref...  16.8 us
    dot_general x1, matrix products, make_attend(): jnp.dot(weights_exp.astype(jnp.bfloat16), incoming[1], preferred_element_...  15.3 us
  transfers between devices with their start and end apart: 8, of which 4 were waited for; matrix products, arithmetic and copies ran while one was open for 9% of the time, Pallas kernels for 0%

commit v1 on v0

v1 whole, which is shorter than its diff:
```python
import functools

import jax
import jax.numpy as jnp
from jax import lax
from jax.experimental import pallas as pl
from jax.experimental.pallas import tpu as pltpu
from jax.sharding import PartitionSpec as P

MESH = pl.DeviceIdType.MESH
F32, BF16 = jnp.float32, jnp.bfloat16
EPS = 1e-06
QSCALE = 24.0 / 128.0 * 1.4426950408889634
N_SEM = 64


def nt_dot(a, b):
    return lax.dot_general(a, b, (((1,), (1,)), ((), ())), preferred_element_type=F32)


def nn_dot(a, b):
    return jnp.dot(a, b, preferred_element_type=F32)


def rms(v):
    return v * lax.rsqrt(jnp.mean(v * v, axis=-1, keepdims=True) + EPS)


def fill(wide, narrow):
    for c in range(3):
        wide[c] = narrow[:, c * 128 : (c + 1) * 128].astype(F32)


def strided(wide, start):
    return jnp.concatenate([wide[c, pl.ds(start, 256, stride=2), :] for c in range(3)], axis=1)


def kernel(
    level_hbm, gain_hbm, wq_hbm, wk_hbm, wv_hbm, wo_hbm, up_hbm, grad_hbm,
    out_ref, gm_ref,
    lv, gain, wq, wk, wv, wo, up, gbuf,
    lv32, g32, xbuf, normed, qall, kva, kvb, acc,
    gm_own, gm_send, gm_recv, o_send, o_recv, r_own, r_send, r_recv,
    mbuf, halo, tbuf, o32,
    load_sem, send_sem, recv_sem,
):
    s = lax.axis_index("seq")
    h = lax.axis_index("head")
    xl, z, y = s // 32, (s // 4) % 8, s % 4

    def at(xl_, z_, y_):
        return ((xl_ * 8 + z_) * 4 + y_, h)

    X = at(1 - xl, z, y)
    ZP, ZM = at(xl, (z + 1) % 8, y), at(xl, (z + 7) % 8, y)
    YP, YM = at(xl, z, (y + 1) % 4), at(xl, z, (y + 3) % 4)
    peers = [(s, (h + j) % 4) for j in (1, 2, 3)]
    nxt, prv = (s + 1) % 64, (s + 63) % 64

    loads = []

    def load(src, dst):
        c = pltpu.make_async_copy(src, dst, load_sem.at[len(loads)])
        c.start()
        loads.append(c)
        return c

    l_lv = load(level_hbm, lv)
    l_g = load(grad_hbm, gbuf.at[pl.ds(16, 512)])
    l_gain = load(gain_hbm, gain)
    l_wk = load(wk_hbm, wk)
    l_wv = load(wv_hbm, wv)
    l_wq = load(wq_hbm, wq)
    l_up = load(up_hbm, up)
    l_wo = load(wo_hbm, wo)

    bar = pltpu.get_barrier_semaphore()
    friends = [X, ZP, ZM, YP, YM] + peers
    friends += [(q, hh) for q in (nxt, prv) for hh in range(4)]
    for f in friends:
        pl.semaphore_signal(bar, inc=1, device_id=f, device_id_type=MESH)

    count = [0]
    sent = []

    def remote(src, dst, dev):
        i = count[0]
        count[0] += 1
        return pltpu.make_async_remote_copy(
            src_ref=src, dst_ref=dst, send_sem=send_sem.at[i], recv_sem=recv_sem.at[i],
            device_id=dev, device_id_type=MESH,
        )

    def send(src, dst, dev):
        c = remote(src, dst, dev)
        c.start()
        sent.append(c)
        return c

    l_lv.wait()
    fill(lv32, lv)
    pooled = 0.5 * (strided(lv32, 0) + strided(lv32, 1))
    xbuf[h] = pooled.astype(BF16)
    l_g.wait()
    pl.semaphore_wait(bar, len(friends))

    c_x = [send(xbuf.at[h], xbuf.at[h], p) for p in peers]
    c_g = [
        send(gbuf.at[pl.ds(512, 16)], gbuf.at[pl.ds(0, 16)], (nxt, h)),
        send(gbuf.at[pl.ds(16, 16)], gbuf.at[pl.ds(528, 16)], (prv, h)),
    ]

    for c in c_g:
        c.wait_recv()
    fill(g32, gbuf)

    @pl.when(s == 0)
    def _():
        g32[:, 0:16, :] = jnp.zeros((3, 16, 128), F32)

    @pl.when(s == 63)
    def _():
        g32[:, 528:544, :] = jnp.zeros((3, 16, 128), F32)

    rows = [strided(g32, 16 + d) for d in range(-2, 4)]
    pair = [(rows[4 - t] + rows[5 - t]).astype(BF16) for t in range(5)]
    l_up.wait()
    for j in (1, 2, 3, 0):
        p = (h + j) % 4
        part = sum(nt_dot(pair[t], up[t, pl.ds(p * 384, 384), :]) for t in range(5))
        if j:
            gm_send[j - 1] = part.astype(BF16)
        else:
            gm_own[...] = part

    for c in c_x:
        c.wait_recv()
    l_gain.wait()
    xs = [xbuf[c].astype(F32) for c in range(4)]
    sq = sum(jnp.sum(v * v, axis=-1, keepdims=True) for v in xs)
    inv = lax.rsqrt(sq / 1536.0 + EPS)
    for c in range(4):
        sl = slice(c * 384, (c + 1) * 384)
        normed[:, sl] = (xs[c] * inv * gain[0:1, sl]).astype(BF16)

    l_wk.wait()
    l_wv.wait()
    mine = normed[pl.ds(pl.multiple_of(h * 64, 64), 64), :]
    kk = rms(nn_dot(mine, wk[...])).astype(BF16)
    vv = nn_dot(mine, wv[...]).astype(BF16)
    one = (lax.broadcasted_iota(jnp.int32, (64, 64), 1) == 0).astype(BF16)
    kv = jnp.concatenate([kk, vv, one], axis=1)

    def sa(xl_, z_, y_):
        return pl.multiple_of(((y_ * 8 + z_) * 2 + xl_) * 32, 32)

    def sb(xl_, z_, y_):
        return pl.multiple_of(((z_ * 4 + y_) * 2 + xl_) * 32, 32)

    def a_rows(start, n):
        return kva.at[pl.ds(start, n)]

    def b_rows(start, n):
        return kvb.at[pl.ds(start, n)]

    own_a, own_b = sa(xl, z, y), sb(xl, z, y)
    kva[pl.ds(own_a, 32), :] = kv[0:32]
    kvb[pl.ds(own_b, 32), :] = kv[32:64]
    c_xa = send(a_rows(own_a, 32), a_rows(own_a, 32), X)
    c_xb = send(b_rows(own_b, 32), b_rows(own_b, 32), X)

    l_wq.wait()
    q = nn_dot(normed[...], wq[...])
    own_q = pl.multiple_of(h * 512, 512)
    for i in range(2):
        qn = rms(q[:, i * 128 : (i + 1) * 128]) * QSCALE
        qall[pl.ds(own_q + i * 256, 256), :] = qn.astype(BF16)
    c_q = [send(qall.at[pl.ds(own_q, 512)], qall.at[pl.ds(own_q, 512)], p) for p in peers]

    def a_pair(z_):
        return a_rows(sa(0, (z_ + 16) % 8, y), 64)

    def b_pair():
        return b_rows(sb(0, z, y), 64)

    def b_group(z_):
        return b_rows(sb(0, (z_ + 16) % 8, 0), 256)

    c_xb.wait_recv()
    c_by = [send(b_pair(), b_pair(), YP), send(b_pair(), b_pair(), YM)]
    c_xa.wait_recv()
    c_ap, c_am = [send(a_pair(z), a_pair(z), ZP)], [send(a_pair(z), a_pair(z), ZM)]
    c_by[0].wait_recv()
    left = b_rows(sb(0, z, (y + 3) % 4), 64)
    c_by2 = send(left, left, YP)
    c_by[1].wait_recv()
    for k in (1, 2, 3):
        c_ap[-1].wait_recv()
        c_ap.append(send(a_pair(z - k), a_pair(z - k), ZP))
        c_am[-1].wait_recv()
        if k < 3:
            c_am.append(send(a_pair(z + k), a_pair(z + k), ZM))
        if k == 1:
            c_by2.wait_recv()
            bp = [remote(b_group(z - i), b_group(z - i), ZP) for i in range(3)]
            bm = [remote(b_group(z + i), b_group(z + i), ZM) for i in range(4)]
            bp[0].start()
            bm[0].start()
    c_ap[-1].wait_recv()

    def a_half(y_, half):
        return a_rows(pl.multiple_of(((y_ + 8) % 4) * 512 + half * 256, 256), 256)

    ar = [remote(a_half(y, i), a_half(y, i), YP) for i in range(2)]
    al = [remote(a_half(y, i), a_half(y, i), YM) for i in range(2)]
    a2r = remote(a_half(y - 1, 0), a_half(y - 1, 0), YP)
    a2l = remote(a_half(y + 1, 1), a_half(y + 1, 1), YM)
    ar[0].start()
    al[1].start()
    ar[1].start()
    al[0].start()
    c_gm = [remote(gm_send.at[j], gm_recv.at[j], peers[j]) for j in range(3)]
    for c in c_q:
        c.wait_recv()
    for c in c_gm:
        c.start()
    acc[...] = jnp.zeros_like(acc)

    @pl.loop(0, 4)
    def _(i):
        @pl.when(i == 0)
        def _():
            bm[0].wait_recv()
            bm[1].start()

        @pl.when(i == 1)
        def _():
            bp[0].wait_recv()
            bp[1].start()
            bm[1].wait_recv()
            bm[2].start()
            al[1].wait_recv()
            a2l.start()
            ar[0].wait_recv()
            a2r.start()
            al[0].wait_recv()

        @pl.when(i == 2)
        def _():
            bp[1].wait_recv()
            bp[2].start()
            bm[2].wait_recv()
            bm[3].start()
            ar[1].wait_recv()

        @pl.when(i == 3)
        def _():
            bp[2].wait_recv()
            bm[3].wait_recv()
            a2r.wait_recv()
            a2l.wait_recv()

        ya = (y + i + i // 2 - 2 * (i // 3)) % 4
        oa = pl.multiple_of(ya * 512, 512)
        ob0 = pl.multiple_of(((z - i + 8) % 8) * 256, 256)
        ob1 = pl.multiple_of(((z + i + 1) % 8) * 256, 256)
        ka = jnp.concatenate(
            [kva[pl.ds(oa, 512), :], kvb[pl.ds(ob0, 256), :], kvb[pl.ds(ob1, 256), :]], axis=0
        )
        keys, vals = ka[:, 0:128], ka[:, 128:384]
        for qi in range(4):
            rs = slice(qi * 512, (qi + 1) * 512)
            w = jnp.exp2(nt_dot(qall[rs, :], keys)).astype(BF16)
            acc[rs, :] += nn_dot(w, vals)

    lane = lax.broadcasted_iota(jnp.int32, (512, 256), 1)
    c_o = []
    for j in (1, 2, 3):
        p = (h + j) % 4
        part = acc[pl.ds(pl.multiple_of(p * 512, 512), 512), :]
        den = part[:, 192:193]
        low = den - den.astype(BF16).astype(F32)
        o_send[j - 1] = jnp.where(lane == 193, low, part).astype(BF16)
        c_o.append(send(o_send.at[j - 1], o_recv.at[j - 1], peers[j - 1]))

    for c in c_gm:
        c.wait_recv()
    gm = gm_own[...]
    for j in range(3):
        gm = gm + gm_recv[j].astype(F32)
    gm_ref[...] = gm.astype(BF16)

    l_wo.wait()
    tot = acc[pl.ds(own_q, 512), :]
    tot = jnp.where(lane == 193, 0.0, tot)
    for c in c_o:
        c.wait_recv()
    for j in range(3):
        tot = tot + o_recv[j].astype(F32)
    den = tot[:, 192:193] + tot[:, 193:194]
    attended = (tot[:, 0:192] / den).astype(BF16)

    c_r = []
    for j in (1, 2, 3, 0):
        p = (h + j) % 4
        col = pl.ds(pl.multiple_of(p * 384, 384), 384)
        part = nn_dot(attended[0:256], wo[0:192, col]) + nn_dot(attended[256:512], wo[192:384, col])
        if j:
            r_send[j - 1] = part.astype(BF16)
            c_r.append(send(r_send.at[j - 1], r_recv.at[j - 1], peers[j - 1]))
        else:
            r_own[...] = part
    total = r_own[...]
    for c in c_r:
        c.wait_recv()
    for j in range(3):
        total = total + r_recv[j].astype(F32)
    mixed = (xbuf[h].astype(F32) + total).astype(BF16)
    mbuf[h] = mixed
    c_m = [send(mbuf.at[h], mbuf.at[h], p) for p in peers]
    halo[0, h] = mixed[240:256]
    halo[1, h] = mixed[0:16]
    c_h = []
    for j in range(4):
        c_h.append(send(halo.at[0, h], halo.at[2, h], (nxt, (h + j) % 4)))
        c_h.append(send(halo.at[1, h], halo.at[3, h], (prv, (h + j) % 4)))

    def conv(t, get):
        return sum(nn_dot(get(c), up[t, c * 384 : (c + 1) * 384, :]) for c in range(4))

    for c in c_m:
        c.wait_recv()
    taps = [conv(t, lambda c: mbuf[c]) for t in range(5)]
    for c in c_h:
        c.wait_recv()
    has_prev = (s > 0).astype(F32)
    has_next = (s < 63).astype(F32)
    lo = [conv(t, lambda c: halo[2, c]) * has_prev for t in (0, 1)]
    hi = [conv(t, lambda c: halo[3, c]) * has_next for t in (3, 4)]

    def shifted(v, before, after, which):
        tbuf[which, 0:16, :] = before
        tbuf[which, 16:272, :] = v
        tbuf[which, 272:288, :] = after

    none = jnp.zeros((16, 384), F32)
    shifted(taps[0] + taps[1], lo[0] + lo[1], none, 0)
    shifted(taps[4], none, hi[1], 1)
    shifted(taps[0], lo[0], none, 2)
    shifted(taps[3] + taps[4], none, hi[0] + hi[1], 3)
    even = tbuf[0, 15:271, :] + (taps[2] + taps[3]) + tbuf[1, 17:273, :]
    odd = tbuf[2, 15:271, :] + (taps[1] + taps[2]) + tbuf[3, 17:273, :]
    for c in range(3):
        lanes = slice(c * 128, (c + 1) * 128)
        o32[c, pl.ds(0, 256, stride=2), :] = even[:, lanes]
        o32[c, pl.ds(1, 256, stride=2), :] = odd[:, lanes]
        out_ref[:, lanes] = (o32[c] + lv32[c]).astype(BF16)

    for c in sent + bp + bm + ar + al + [a2r, a2l] + c_gm:
        c.wait_send()


def per_device(level_input, norm_gain, query_weight, key_weight, value_weight, out_weight, up_weight, grad_output):
    any_spec = pl.BlockSpec(memory_space=pl.ANY)
    vmem = pl.BlockSpec(memory_space=pltpu.VMEM)
    v = pltpu.VMEM
    return pl.pallas_call(
        kernel,
        out_shape=(
            jax.ShapeDtypeStruct((512, 384), BF16),
            jax.ShapeDtypeStruct((256, 384), BF16),
        ),
        in_specs=[any_spec] * 8,
        out_specs=(vmem, vmem),
        scratch_shapes=[
            v((512, 384), BF16), v((1, 1536), F32), v((1536, 256), BF16), v((1536, 128), BF16),
            v((1536, 192), BF16), v((384, 1536), BF16), v((5, 1536, 384), BF16), v((544, 384), BF16),
            v((3, 512, 128), F32), v((3, 544, 128), F32), v((4, 256, 384), BF16), v((256, 1536), BF16),
            v((2048, 128), BF16), v((2048, 384), BF16), v((2048, 384), BF16), v((2048, 256), F32),
            v((256, 384), F32), v((3, 256, 384), BF16), v((3, 256, 384), BF16),
            v((3, 512, 256), BF16), v((3, 512, 256), BF16),
            v((256, 384), F32), v((3, 256, 384), BF16), v((3, 256, 384), BF16),
            v((4, 256, 384), BF16), v((4, 4, 16, 384), BF16), v((4, 288, 384), F32), v((3, 512, 128), F32),
            pltpu.SemaphoreType.DMA((8,)),
            pltpu.SemaphoreType.DMA((N_SEM,)),
            pltpu.SemaphoreType.DMA((N_SEM,)),
        ],
        compiler_params=pltpu.CompilerParams(
            collective_id=0, has_side_effects=True, vmem_limit_bytes=56 << 20
        ),
    )(
        level_input, norm_gain.reshape(1, -1), query_weight, key_weight, value_weight,
        out_weight, up_weight, grad_output,
    )


def solution(mesh):
    in_specs = (
        P("seq", "head"), P(), P(None, "head"), P(), P(), P("head", None),
        P(None, None, "head"), P("seq", "head"),
    )
    out_specs = (P("seq", "head"), P("seq", "head"))
    return jax.shard_map(
        per_device, mesh=mesh, in_specs=in_specs, out_specs=out_specs, check_vma=False
    )
```

time: 663 us -> 107 us (0.16)
  waiting for transfers between devices: 507 us -> 0 us
  Pallas kernels: 0 us -> 98.8 us
  matrix products: 71.7 us -> 0 us
  local copies, waits for them, and re-layouts: 34.3 us -> 6.92 us
  blocking collectives: 22.3 us -> 0 us
  between operations: 14.1 us -> 0.64 us
  starting transfers between devices: 10 us -> 0 us
    all_gather x2 -> x0, waiting for transfers between devices: 431 us -> none  [the longest x1 238 us: per_device(): lax.all_gather(value_local, 'seq', axis=0, tiled=True)]
    pallas_call x0 -> x1, Pallas kernels: none -> 98.8 us  [per_device(): pl.pallas_call(kernel, out_shape=(jax.ShapeDtypeStruct((512, 384), BF16),...]
    unnamed x6 -> x0, waiting for transfers between devices: 76.2 us -> none
    dot_general x16 -> x0, matrix products: 71.7 us -> none  [the longest x6 35.8 us: contract_last(): lax.dot_general(left, right, (((1,), (1,)), ((), ())), preferred_element_...]
    slice x10 -> x0, local copies, waits for them, and re-layouts: 23.2 us -> none  [the longest x2 13.2 us: per_device(): paired = grad_upsampled[0::2] + grad_upsampled[1::2]]
    all_gather x2 -> x0, blocking collectives: 22.3 us -> none  [the longest x1 11.9 us: per_device(): gathered = lax.all_gather(pooled, 'head', axis=1, tiled=True)]
    ppermute x4 -> x0, starting transfers between devices: 9.68 us -> none  [the longest x2 7.1 us: with_halo(): lax.ppermute(lax.slice_in_dim(block, block.shape[dim] - width, None, axis...]
  transfers between devices with their start and end apart: 8 -> 0, of which waited for: 4 -> 0; matrix products, arithmetic and copies ran while one was open for 9% -> 0% of each run, Pallas kernels for 0% -> 0%
where the time goes in v1:
time: 107 us; the launch traced here: 106 us
  Pallas kernels  98.8 us (92%)
  local copies, waits for them, and re-layouts  6.92 us (6%)
    pallas_call x1, Pallas kernels, per_device(): pl.pallas_call(kernel, out_shape=(jax.ShapeDtypeStruct((512, 384), BF16),...  98.8 us
    unnamed x3, local copies, waits for them, and re-layouts  5.62 us

profile of v1, /device:TPU:1, one launch (start us, length us, event | category | flops | bytes accessed | tf_op | source)
XLA Modules:
  0.0 106.3 jit_solution(15563989416115564562)
XLA Ops:
  0.6 1.3 %reshape.7.gain_hbm = f32[1,1536]{1,0:T(1,128)} reshape(f32[1536]{0:T(1024)} %param.9) | data formatting | bytes 12288 | tf_op jit(solution)/shard_map/reshape | solution.py:392
  1.9 2.2 %copy.10.wv_hbm = bf16[1536,192]{1,0:T(8,128)(2,1)} copy(bf16[1536,192]{0,1:T(8,128)(2,1)} %param.12) | data formatting | bytes 1179648 | tf_op args[4]
  4.1 98.8 %shard_map.95 = (bf16[512,384]{1,0:T(8,128)(2,1)}, bf16[256,384]{1,0:T(8,128)(2,1)}) custom-call(bf16[512,384]{1,0:T(8,128)(2,1)} %level_hbm.1, f32[1,1536]{1,0:T(1,128)} %reshape.7.gain_hbm, bf16[1536,256]{1,0:T(8,128)(2,1)} %wq_hbm.1, bf16[1536,128]{1,0:T(8,128)(2,1)} %wk_hbm.1, bf16[1536,192]{1,0:T(8,128)(2,1)} %copy.10.wv_hbm, bf16[384,1536]{1,0:T(8,128)(2,1)} %wo_hbm.1, ...), custom_call_target="tpu_custom_call" | custom-call | tf_op jit(solution)/shard_map/pallas_call | solution.py:367
  102.9 1.8 %copy.13 = bf16[512,384]{1,0:T(8,128)(2,1)} copy(bf16[512,384]{1,0:T(8,128)(2,1)} %get-tuple-element.4) | data formatting | bytes 786432
  104.7 1.6 %copy.14 = bf16[256,384]{1,0:T(8,128)(2,1)} copy(bf16[256,384]{1,0:T(8,128)(2,1)} %get-tuple-element.5) | data formatting | bytes 393216

commit v2 on v1

v2 whole, which is shorter than its diff:
```python
import functools

import jax
import jax.numpy as jnp
from jax import lax
from jax.experimental import pallas as pl
from jax.experimental.pallas import tpu as pltpu
from jax.sharding import PartitionSpec as P

MESH = pl.DeviceIdType.MESH
F32, BF16 = jnp.float32, jnp.bfloat16
EPS = 1e-06
QSCALE = 24.0 / 128.0 * 1.4426950408889634
N_SEM = 128
RA, RB = 48, 16


def nt_dot(a, b):
    return lax.dot_general(a, b, (((1,), (1,)), ((), ())), preferred_element_type=F32)


def nn_dot(a, b):
    return jnp.dot(a, b, preferred_element_type=F32)


def rms(v):
    return v * lax.rsqrt(jnp.mean(v * v, axis=-1, keepdims=True) + EPS)


def fill(wide, narrow):
    for c in range(3):
        wide[c] = narrow[:, c * 128 : (c + 1) * 128].astype(F32)


def strided(wide, start):
    return jnp.concatenate([wide[c, pl.ds(start, 256, stride=2), :] for c in range(3)], axis=1)


def kernel(
    level_hbm, gain_hbm, wq_hbm, wk_hbm, wv_hbm, wo_hbm, up_hbm, grad_hbm,
    out_ref, gm_ref,
    lv, gain, wq, wk, wv, wo, up, gbuf,
    lv32, g32, xbuf, xq, normed, qall, kva, kvb, acc,
    gm_own, gm_send, gm_recv, o_send, o_recv, mbuf, halo, tbuf, o32,
    load_sem, send_sem, recv_sem,
):
    s = lax.axis_index("seq")
    h = lax.axis_index("head")
    xl, z, y = s // 32, (s // 4) % 8, s % 4
    hs = h + 1 - 2 * (h % 2)
    hx = (h + 2) % 4
    hd = (hs + 2) % 4

    def at(xl_, z_, y_):
        return ((xl_ * 8 + z_) * 4 + y_, h)

    X = at(1 - xl, z, y)
    ZP, ZM = at(xl, (z + 1) % 8, y), at(xl, (z + 7) % 8, y)
    YP, YM = at(xl, z, (y + 1) % 4), at(xl, z, (y + 3) % 4)
    SIB, XH, DIAG = (s, hs), (s, hx), (s, hd)
    XLH = (X[0], hx)
    NXT, PRV = ((s + 1) % 64, h), ((s + 63) % 64, h)

    loads = []

    def load(src, dst):
        c = pltpu.make_async_copy(src, dst, load_sem.at[len(loads)])
        c.start()
        loads.append(c)
        return c

    l_lv = load(level_hbm, lv)
    l_g = load(grad_hbm, gbuf.at[pl.ds(16, 512)])
    l_gain = load(gain_hbm, gain)
    l_wk = load(wk_hbm, wk)
    l_wv = load(wv_hbm, wv)
    l_wq = load(wq_hbm, wq)
    l_up = load(up_hbm, up)
    l_wo = load(wo_hbm, wo.at[h])

    bar = pltpu.get_barrier_semaphore()
    friends = [X, ZP, ZM, YP, YM, SIB, XH, DIAG, XLH, NXT, PRV]
    for f in friends:
        pl.semaphore_signal(bar, inc=1, device_id=f, device_id_type=MESH)

    count = [0]
    sent = []

    def remote(src, dst, dev):
        i = count[0]
        count[0] += 1
        c = pltpu.make_async_remote_copy(
            src_ref=src, dst_ref=dst, send_sem=send_sem.at[i], recv_sem=recv_sem.at[i],
            device_id=dev, device_id_type=MESH,
        )
        sent.append(c)
        return c

    def send(src, dst, dev):
        c = remote(src, dst, dev)
        c.start()
        return c

    def push(ref, dev):
        return send(ref, ref, dev)

    l_lv.wait()
    fill(lv32, lv)
    pooled = 0.5 * (strided(lv32, 0) + strided(lv32, 1))
    xbuf[h] = pooled.astype(BF16)
    l_g.wait()
    own64 = pl.ds(pl.multiple_of(h * 64, 64), 64)
    xq[h] = xbuf[h, own64, :]
    pl.semaphore_wait(bar, len(friends))

    def quarter(p, dev):
        return send(xbuf.at[h, pl.ds(pl.multiple_of(p * 64, 64), 64)], xq.at[h], dev)

    c_quarter = [quarter(hx, XH), quarter(hd, DIAG), quarter(hs, SIB)]
    c_g = [
        send(gbuf.at[pl.ds(512, 16)], gbuf.at[pl.ds(0, 16)], NXT),
        send(gbuf.at[pl.ds(16, 16)], gbuf.at[pl.ds(528, 16)], PRV),
    ]
    x_x = push(xbuf.at[h], XH)
    x_s = push(xbuf.at[h], SIB)

    def normalize(blocks, store):
        sq = sum(jnp.sum(v * v, axis=-1, keepdims=True) for v in blocks)
        inv = lax.rsqrt(sq / 1536.0 + EPS)
        for c in range(4):
            sl = slice(c * 384, (c + 1) * 384)
            store(sl, (blocks[c] * inv * gain[sl].reshape(1, 384)).astype(BF16))

    l_gain.wait()
    l_wk.wait()
    l_wv.wait()
    for c in c_quarter:
        c.wait_recv()
    mine = []
    normalize([xq[c].astype(F32) for c in range(4)], lambda sl, v: mine.append(v))
    mine = jnp.concatenate(mine, axis=1)
    kk = rms(nn_dot(mine, wk[...])).astype(BF16)
    vv = nt_dot(mine, wv[...]).astype(BF16)
    one = (lax.broadcasted_iota(jnp.int32, (64, 64), 1) == 0).astype(BF16)
    kv = jnp.concatenate([kk, vv, one], axis=1)

    def pa(z_, y_, n=1):
        start = (((y_ + 4) % 4) * 8 + (z_ + 8) % 8) * 2 * RA
        return kva.at[pl.ds(pl.multiple_of(start, 2 * RA), 2 * RA)]

    def pb(z_, y_):
        start = (((z_ + 8) % 8) * 4 + (y_ + 4) % 4) * 2 * RB
        return kvb.at[pl.ds(pl.multiple_of(start, 2 * RB), 2 * RB)]

    def gb(z_):
        return kvb.at[pl.ds(pl.multiple_of(((z_ + 8) % 8) * 8 * RB, 8 * RB), 8 * RB)]

    own_a = pl.ds(pl.multiple_of(((y * 8 + z) * 2 + xl) * RA, RA), RA)
    own_b = pl.ds(pl.multiple_of(((z * 4 + y) * 2 + xl) * RB, RB), RB)
    kva[own_a, :] = kv[0:RA]
    kvb[own_b, :] = kv[RA:64]
    c_xa = push(kva.at[own_a], X)
    c_xb = push(kvb.at[own_b], X)

    for c in c_g:
        c.wait_recv()
    fill(g32, gbuf)

    @pl.when(s == 0)
    def _():
        g32[:, 0:16, :] = jnp.zeros((3, 16, 128), F32)

    @pl.when(s == 63)
    def _():
        g32[:, 528:544, :] = jnp.zeros((3, 16, 128), F32)

    rows = [strided(g32, 16 + d) for d in range(-2, 4)]
    pair = [(rows[4 - t] + rows[5 - t]).astype(BF16) for t in range(5)]

    c_xa.wait_recv()
    zr, zl = [push(pa(z, y), ZP)], [push(pa(z, y), ZM)]
    yr, yl = {0: push(pa(z, y), YP)}, {0: push(pa(z, y), YM)}
    c_xb.wait_recv()
    by = [push(pb(z, y), YP), push(pb(z, y), YM)]
    x_x.wait_recv()
    x_f = push(xbuf.at[hx], SIB)
    wo_rows = [slice(0, 128), slice(128, 256), slice(256, 384)]
    l_wo.wait()
    wo_x = [push(wo.at[h, r], XLH) for r in wo_rows]
    wo_s = [push(wo.at[h, r], SIB) for r in wo_rows]

    def grad_block(p):
        return sum(nt_dot(pair[t], up[t, pl.ds(p * 384, 384), :]) for t in range(5))

    def step(k):
        zr[-1].wait_recv()
        if k < 4:
            zr.append(push(pa(z - k, y), ZP))
        yr[-k] = push(pa(z - k, y), YP)
        yl[-k] = push(pa(z - k, y), YM)
        if k < 4:
            zl[-1].wait_recv()
            if k < 3:
                zl.append(push(pa(z + k, y), ZM))
            yr[k] = push(pa(z + k, y), YP)
            yl[k] = push(pa(z + k, y), YM)

    yr2, yl2 = [], []

    def turn(d):
        if d in (0, -1, -2, -3):
            yr[d].wait_recv()
            yr2.append(push(pa(z + d, y - 1), YP))
        else:
            yl[d].wait_recv()
            yl2.append(push(pa(z + d, y + 1), YM))

    l_up.wait()
    gm_send[0] = grad_block(hd).astype(BF16)
    gm_send[1] = grad_block(hs).astype(BF16)
    step(1)
    by[0].wait_recv()
    by2 = push(pb(z, y - 1), YP)
    turn(0)

    x_s.wait_recv()
    x_f.wait_recv()

    def put(sl, v):
        normed[:, sl] = v

    normalize([xbuf[c].astype(F32) for c in range(4)], put)
    l_wq.wait()
    q = nn_dot(normed[...], wq[...])
    for i in range(2):
        qn = (rms(q[:, i * 128 : (i + 1) * 128]) * QSCALE).astype(BF16)
        for p in range(4):
            qall[p, 2 * h + i] = qn[p * 64 : (p + 1) * 64]

    def heads(c):
        return qall.at[:, pl.ds(2 * c, 2)]

    q_x = push(heads(h), XH)
    q_s = push(heads(h), SIB)
    step(2)
    by[1].wait_recv()
    by2.wait_recv()
    bp = [remote(gb(z - i), gb(z - i), ZP) for i in range(3)]
    bm = [remote(gb(z + i), gb(z + i), ZM) for i in range(4)]
    bp[0].start()
    bm[0].start()
    turn(-1)
    turn(1)
    gm_own[0] = grad_block(hx)
    step(3)
    turn(-2)
    turn(2)
    q_x.wait_recv()
    q_f = push(heads(hx), SIB)
    gm_1 = [send(gm_send.at[i], gm_recv.at[i], SIB) for i in range(2)]
    gm_own[1] = grad_block(h)
    step(4)
    turn(-3)
    turn(3)
    acc[...] = jnp.zeros_like(acc)
    q_s.wait_recv()
    q_f.wait_recv()
    gm_2 = remote(gm_send.at[2], gm_recv.at[2], XH)

    def keys_values(i):
        ya = (y + i + i // 2 - 2 * (i // 3)) % 4
        oa = pl.multiple_of(ya * 16 * RA, 16 * RA)
        ob0 = pl.multiple_of(((z - i + 8) % 8) * 8 * RB, 8 * RB)
        ob1 = pl.multiple_of(((z + i + 1) % 8) * 8 * RB, 8 * RB)
        ka = jnp.concatenate(
            [kva[pl.ds(oa, 16 * RA), :], kvb[pl.ds(ob0, 8 * RB), :], kvb[pl.ds(ob1, 8 * RB), :]],
            axis=0,
        )
        return ka[:, 0:128], ka[:, 128:384]

    def attend(p, keys, vals):
        w = jnp.exp2(nt_dot(qall[p].reshape(512, 128), keys)).astype(BF16)
        return nn_dot(w, vals)

    yr2_3 = pa(z - 4, y + 1)
    last_l = remote(yr2_3, yr2_3, YM)

    @pl.loop(0, 3)
    def _(i):
        @pl.when(i == 0)
        def _():
            bm[0].wait_recv()
            bm[1].start()
            bp[0].wait_recv()
            bp[1].start()

        @pl.when(i == 1)
        def _():
            yl[-4].wait_recv()
            last_l.start()
            for d in (0, -1, -2, -3):
                yl[d].wait_recv()
            bm[1].wait_recv()
            bm[2].start()
            gm_1[0].wait_recv()
            gm_send[2] = (gm_own[0] + gm_recv[0].astype(F32)).astype(BF16)
            gm_2.start()

        @pl.when(i == 2)
        def _():
            for d in (1, 2, 3, -4):
                yr[d].wait_recv()
            bp[1].wait_recv()
            bp[2].start()
            bm[2].wait_recv()
            bm[3].start()

        keys, vals = keys_values(i)
        for p in range(4):
            acc[p] += attend(p, keys, vals)

    for c in yr2 + yl2 + [last_l, bp[2], bm[3]]:
        c.wait_recv()
    keys, vals = keys_values(3)
    lane = lax.broadcasted_iota(jnp.int32, (512, 256), 1)

    def packed(part):
        den = part[:, 192:193]
        low = den - den.astype(BF16).astype(F32)
        return jnp.where(lane == 193, low, part).astype(BF16)

    o_1 = []
    for i, p in enumerate((hd, hs)):
        o_send[i] = packed(acc[p] + attend(p, keys, vals))
        o_1.append(send(o_send.at[i], o_recv.at[i], SIB))
    for p in (hx, h):
        acc[p] += attend(p, keys, vals)

    def clear(part):
        return jnp.where(lane == 193, 0.0, part)

    def widen(part):
        part = part.astype(F32)
        return jnp.where(lane == 192, part + part[:, 193:194], clear(part))

    o_1[0].wait_recv()
    o_send[2] = packed(clear(acc[hx]) + widen(o_recv[0]))
    o_2 = send(o_send.at[2], o_recv.at[2], XH)

    wo_f = []
    for i, r in enumerate(wo_rows):
        wo_x[i].wait_recv()
        wo_f.append(push(wo.at[hx, r], SIB))

    o_1[1].wait_recv()
    tot = clear(acc[h]) + widen(o_recv[1])
    gm_1[1].wait_recv()
    gm_2.wait_recv()
    gm_ref[...] = (gm_own[1] + gm_recv[1].astype(F32) + gm_recv[2].astype(F32)).astype(BF16)
    for c in wo_s + wo_f:
        c.wait_recv()
    o_2.wait_recv()
    tot = tot + widen(o_recv[2])
    att = (tot[:, 0:192] / tot[:, 192:193]).astype(BF16)
    att = jnp.concatenate([att[g * 64 : (g + 1) * 64] for g in range(8)], axis=1)
    mixed = jnp.concatenate([xq[c] for c in range(4)], axis=1).astype(F32)
    for c in range(4):
        mixed = mixed + nn_dot(att[:, c * 384 : (c + 1) * 384], wo[c])
    mbuf[h] = mixed.astype(BF16)
    m_x = push(mbuf.at[h], XH)
    m_s = push(mbuf.at[h], SIB)
    m_x.wait_recv()
    m_f = push(mbuf.at[hx], SIB)
    m_s.wait_recv()
    m_f.wait_recv()
    c_h = [
        send(mbuf.at[3, pl.ds(48, 16)], halo.at[0], NXT),
        send(mbuf.at[0, pl.ds(0, 16)], halo.at[1], PRV),
    ]

    full = mbuf[...].reshape(256, 1536)
    taps = [nn_dot(full, up[t]) for t in range(5)]
    for c in c_h:
        c.wait_recv()
    has_prev = (s > 0).astype(F32)
    has_next = (s < 63).astype(F32)
    lo = [nn_dot(halo[0], up[t]) * has_prev for t in (0, 1)]
    hi = [nn_dot(halo[1], up[t]) * has_next for t in (3, 4)]

    def shifted(v, before, after, which):
        tbuf[which, 0:16, :] = before
        tbuf[which, 16:272, :] = v
        tbuf[which, 272:288, :] = after

    none = jnp.zeros((16, 384), F32)
    shifted(taps[0] + taps[1], lo[0] + lo[1], none, 0)
    shifted(taps[4], none, hi[1], 1)
    shifted(taps[0], lo[0], none, 2)
    shifted(taps[3] + taps[4], none, hi[0] + hi[1], 3)
    even = tbuf[0, 15:271, :] + (taps[2] + taps[3]) + tbuf[1, 17:273, :]
    odd = tbuf[2, 15:271, :] + (taps[1] + taps[2]) + tbuf[3, 17:273, :]
    for c in range(3):
        lanes = slice(c * 128, (c + 1) * 128)
        o32[c, pl.ds(0, 256, stride=2), :] = even[:, lanes]
        o32[c, pl.ds(1, 256, stride=2), :] = odd[:, lanes]
        out_ref[:, lanes] = (o32[c] + lv32[c]).astype(BF16)

    for c in sent:
        c.wait_send()


def per_device(level_input, norm_gain, query_weight, key_weight, value_weight, out_weight, up_weight, grad_output):
    any_spec = pl.BlockSpec(memory_space=pl.ANY)
    vmem = pl.BlockSpec(memory_space=pltpu.VMEM)
    v = pltpu.VMEM
    outs = pl.pallas_call(
        kernel,
        out_shape=(
            jax.ShapeDtypeStruct((512, 384), BF16),
            jax.ShapeDtypeStruct((256, 384), BF16),
        ),
        in_specs=[any_spec] * 8,
        out_specs=(vmem, vmem),
        scratch_shapes=[
            v((512, 384), BF16), v((1536,), F32), v((1536, 256), BF16), v((1536, 128), BF16),
            v((192, 1536), BF16), v((4, 384, 1536), BF16), v((5, 1536, 384), BF16), v((544, 384), BF16),
            v((3, 512, 128), F32), v((3, 544, 128), F32), v((4, 256, 384), BF16), v((4, 64, 384), BF16),
            v((256, 1536), BF16), v((4, 8, 64, 128), BF16), v((64 * RA, 384), BF16),
            v((64 * RB, 384), BF16), v((4, 512, 256), F32),
            v((2, 256, 384), F32), v((3, 256, 384), BF16), v((3, 256, 384), BF16),
            v((3, 512, 256), BF16), v((3, 512, 256), BF16),
            v((4, 64, 1536), BF16), v((2, 16, 1536), BF16), v((4, 288, 384), F32), v((3, 512, 128), F32),
            pltpu.SemaphoreType.DMA((8,)),
            pltpu.SemaphoreType.DMA((N_SEM,)),
            pltpu.SemaphoreType.DMA((N_SEM,)),
        ],
        compiler_params=pltpu.CompilerParams(
            collective_id=0, has_side_effects=True, vmem_limit_bytes=56 << 20
        ),
    )(
        level_input, norm_gain, query_weight, key_weight, value_weight.T,
        out_weight, up_weight, grad_output,
    )
    return outs


def solution(mesh):
    in_specs = (
        P("seq", "head"), P(), P(None, "head"), P(), P(), P("head", None),
        P(None, None, "head"), P("seq", "head"),
    )
    out_specs = (P("seq", "head"), P("seq", "head"))
    return jax.shard_map(
        per_device, mesh=mesh, in_specs=in_specs, out_specs=out_specs, check_vma=False
    )
```

time: 107 us -> 82.5 us (0.77)
  Pallas kernels: 98.8 us -> 78.3 us
  local copies, waits for them, and re-layouts: 6.92 us -> 3.4 us
    pallas_call x1, Pallas kernels: 98.8 us -> 78.3 us  [per_device(): pl.pallas_call(kernel, out_shape=(jax.ShapeDtypeStruct((512, 384), BF16),...]
    unnamed x3 -> x2, local copies, waits for them, and re-layouts: 5.62 us -> 3.4 us
    reshape x1 -> x0, local copies, waits for them, and re-layouts: 1.3 us -> none  [per_device(): norm_gain.reshape(1, -1)]
where the time goes in v2:
time: 82.5 us; the launch traced here: 82.4 us
  Pallas kernels  78.3 us (95%)
  local copies, waits for them, and re-layouts  3.4 us (4%)
    pallas_call x1, Pallas kernels, per_device(): pl.pallas_call(kernel, out_shape=(jax.ShapeDtypeStruct((512, 384), BF16),...  78.3 us
    unnamed x2, local copies, waits for them, and re-layouts  3.4 us

profile of v2, /device:TPU:1, one launch (start us, length us, event | category | flops | bytes accessed | tf_op | source)
XLA Modules:
  0.0 82.4 jit_solution(16244286786259133000)
XLA Ops:
  0.6 78.3 %shard_map.95 = (bf16[512,384]{1,0:T(8,128)(2,1)}, bf16[256,384]{1,0:T(8,128)(2,1)}) custom-call(bf16[512,384]{1,0:T(8,128)(2,1)} %level_hbm.1, f32[1536]{0:T(1024)} %gain_hbm.1, bf16[1536,256]{1,0:T(8,128)(2,1)} %wq_hbm.1, bf16[1536,128]{1,0:T(8,128)(2,1)} %wk_hbm.1, bf16[192,1536]{1,0:T(8,128)(2,1)} %bitcast.1, bf16[384,1536]{1,0:T(8,128)(2,1)} %wo_hbm.1, ...), custom_call_target="tpu_custom_call" | custom-call | tf_op jit(solution)/shard_map/pallas_call | solution.py:416
  79.0 1.8 %copy.12 = bf16[512,384]{1,0:T(8,128)(2,1)} copy(bf16[512,384]{1,0:T(8,128)(2,1)} %get-tuple-element.4) | data formatting | bytes 786432
  80.8 1.6 %copy.13 = bf16[256,384]{1,0:T(8,128)(2,1)} copy(bf16[256,384]{1,0:T(8,128)(2,1)} %get-tuple-element.5) | data formatting | bytes 393216

commit v3 on v2

--- a/solution.py
+++ b/solution.py
@@ -40,7 +40,7 @@
     level_hbm, gain_hbm, wq_hbm, wk_hbm, wv_hbm, wo_hbm, up_hbm, grad_hbm,
     out_ref, gm_ref,
     lv, gain, wq, wk, wv, wo, up, gbuf,
-    lv32, g32, xbuf, xq, normed, qall, kva, kvb, acc,
+    lv32, g32, xbuf, xq, normed, qall, kvx, kva, kvb, acc,
     gm_own, gm_send, gm_recv, o_send, o_recv, mbuf, halo, tbuf, o32,
     load_sem, send_sem, recv_sem,
 ):
@@ -144,23 +144,17 @@
     one = (lax.broadcasted_iota(jnp.int32, (64, 64), 1) == 0).astype(BF16)
     kv = jnp.concatenate([kk, vv, one], axis=1)
 
-    def pa(z_, y_, n=1):
-        start = (((y_ + 4) % 4) * 8 + (z_ + 8) % 8) * 2 * RA
-        return kva.at[pl.ds(pl.multiple_of(start, 2 * RA), 2 * RA)]
+    def pa(z_, y_):
+        return kva.at[((y_ + 4) % 4) * 8 + (z_ + 8) % 8]
 
     def pb(z_, y_):
-        start = (((z_ + 8) % 8) * 4 + (y_ + 4) % 4) * 2 * RB
-        return kvb.at[pl.ds(pl.multiple_of(start, 2 * RB), 2 * RB)]
+        return kvb.at[((z_ + 8) % 8) * 4 + (y_ + 4) % 4]
 
     def gb(z_):
-        return kvb.at[pl.ds(pl.multiple_of(((z_ + 8) % 8) * 8 * RB, 8 * RB), 8 * RB)]
-
-    own_a = pl.ds(pl.multiple_of(((y * 8 + z) * 2 + xl) * RA, RA), RA)
-    own_b = pl.ds(pl.multiple_of(((z * 4 + y) * 2 + xl) * RB, RB), RB)
-    kva[own_a, :] = kv[0:RA]
-    kvb[own_b, :] = kv[RA:64]
-    c_xa = push(kva.at[own_a], X)
-    c_xb = push(kvb.at[own_b], X)
+        return kvb.at[pl.ds(((z_ + 8) % 8) * 4, 4)]
+
+    kvx[xl] = kv
+    c_x = push(kvx.at[xl], X)
 
     for c in c_g:
         c.wait_recv()
@@ -177,10 +171,20 @@
     rows = [strided(g32, 16 + d) for d in range(-2, 4)]
     pair = [(rows[4 - t] + rows[5 - t]).astype(BF16) for t in range(5)]
 
-    c_xa.wait_recv()
+    c_x.wait_recv()
+
+    def pack(dst, slot, first, n):
+        left, right = kvx[0, first : first + n, :], kvx[1, first : first + n, :]
+        dst[slot, 0:n] = left[:, 0:128]
+        dst[slot, n : 2 * n] = right[:, 0:128]
+        dst[slot, 2 * n : 3 * n] = left[:, 128:256]
+        dst[slot, 3 * n : 4 * n] = right[:, 128:256]
+        dst[slot, 4 * n : 5 * n] = jnp.concatenate([left[:, 256:320], right[:, 256:320]], axis=1)
+
+    pack(kva, y * 8 + z, 0, RA)
+    pack(kvb, z * 4 + y, RA, RB)
     zr, zl = [push(pa(z, y), ZP)], [push(pa(z, y), ZM)]
     yr, yl = {0: push(pa(z, y), YP)}, {0: push(pa(z, y), YM)}
-    c_xb.wait_recv()
     by = [push(pb(z, y), YP), push(pb(z, y), YM)]
     x_x.wait_recv()
     x_f = push(xbuf.at[hx], SIB)
@@ -269,14 +273,22 @@
 
     def keys_values(i):
         ya = (y + i + i // 2 - 2 * (i // 3)) % 4
-        oa = pl.multiple_of(ya * 16 * RA, 16 * RA)
-        ob0 = pl.multiple_of(((z - i + 8) % 8) * 8 * RB, 8 * RB)
-        ob1 = pl.multiple_of(((z + i + 1) % 8) * 8 * RB, 8 * RB)
-        ka = jnp.concatenate(
-            [kva[pl.ds(oa, 16 * RA), :], kvb[pl.ds(ob0, 8 * RB), :], kvb[pl.ds(ob1, 8 * RB), :]],
-            axis=0,
-        )
-        return ka[:, 0:128], ka[:, 128:384]
+        keys, vals = [], []
+        for group, n in (
+            (kva[pl.ds(ya * 8, 8)], RA),
+            (kvb[pl.ds(((z - i + 8) % 8) * 4, 4)], RB),
+            (kvb[pl.ds(((z + i + 1) % 8) * 4, 4)], RB),
+        ):
+            slots = group.shape[0]
+            rest = group[:, 4 * n : 5 * n]
+            turned = jnp.concatenate([rest[:, :, 64:128], rest[:, :, 0:64]], axis=2)
+            rest = jnp.concatenate([rest, turned], axis=1).reshape(slots * 2 * n, 128)
+            at_lane = lax.broadcasted_iota(jnp.int32, rest.shape, 1)
+            rest = jnp.where(at_lane < 64, rest, (at_lane == 64).astype(BF16))
+            keys.append(group[:, 0 : 2 * n].reshape(slots * 2 * n, 128))
+            first = group[:, 2 * n : 4 * n].reshape(slots * 2 * n, 128)
+            vals.append(jnp.concatenate([first, rest], axis=1))
+        return jnp.concatenate(keys, axis=0), jnp.concatenate(vals, axis=0)
 
     def attend(p, keys, vals):
         w = jnp.exp2(nt_dot(qall[p].reshape(512, 128), keys)).astype(BF16)
@@ -284,6 +296,8 @@
 
     yr2_3 = pa(z - 4, y + 1)
     last_l = remote(yr2_3, yr2_3, YM)
+
+    wo_f = [remote(wo.at[hx, r], wo.at[hx, r], SIB) for r in wo_rows]
 
     @pl.loop(0, 3)
     def _(i):
@@ -305,9 +319,13 @@
             gm_1[0].wait_recv()
             gm_send[2] = (gm_own[0] + gm_recv[0].astype(F32)).astype(BF16)
             gm_2.start()
+            wo_x[0].wait_recv()
+            wo_f[0].start()
 
         @pl.when(i == 2)
         def _():
+            wo_x[1].wait_recv()
+            wo_f[1].start()
             for d in (1, 2, 3, -4):
                 yr[d].wait_recv()
             bp[1].wait_recv()
@@ -347,10 +365,8 @@
     o_send[2] = packed(clear(acc[hx]) + widen(o_recv[0]))
     o_2 = send(o_send.at[2], o_recv.at[2], XH)
 
-    wo_f = []
-    for i, r in enumerate(wo_rows):
-        wo_x[i].wait_recv()
-        wo_f.append(push(wo.at[hx, r], SIB))
+    wo_x[2].wait_recv()
+    wo_f[2].start()
 
     o_1[1].wait_recv()
     tot = clear(acc[h]) + widen(o_recv[1])
@@ -363,29 +379,39 @@
     tot = tot + widen(o_recv[2])
     att = (tot[:, 0:192] / tot[:, 192:193]).astype(BF16)
     att = jnp.concatenate([att[g * 64 : (g + 1) * 64] for g in range(8)], axis=1)
-    mixed = jnp.concatenate([xq[c] for c in range(4)], axis=1).astype(F32)
-    for c in range(4):
-        mixed = mixed + nn_dot(att[:, c * 384 : (c + 1) * 384], wo[c])
-    mbuf[h] = mixed.astype(BF16)
-    m_x = push(mbuf.at[h], XH)
-    m_s = push(mbuf.at[h], SIB)
-    m_x.wait_recv()
-    m_f = push(mbuf.at[hx], SIB)
-    m_s.wait_recv()
-    m_f.wait_recv()
-    c_h = [
-        send(mbuf.at[3, pl.ds(48, 16)], halo.at[0], NXT),
-        send(mbuf.at[0, pl.ds(0, 16)], halo.at[1], PRV),
-    ]
-
-    full = mbuf[...].reshape(256, 1536)
-    taps = [nn_dot(full, up[t]) for t in range(5)]
+    pooled = jnp.concatenate([xq[c] for c in range(4)], axis=1).astype(F32)
+    m_x, m_s, m_f = [], [], []
+    for c in range(3):
+        col = slice(c * 512, (c + 1) * 512)
+        part = pooled[:, col]
+        for b in range(4):
+            part = part + nn_dot(att[:, b * 384 : (b + 1) * 384], wo[b, :, col])
+        mbuf[c, h] = part.astype(BF16)
+        m_x.append(push(mbuf.at[c, h], XH))
+        m_s.append(push(mbuf.at[c, h], SIB))
+    for c in range(3):
+        m_x[c].wait_recv()
+        m_f.append(push(mbuf.at[c, hx], SIB))
+    c_h = []
+    taps = [0.0] * 5
+    for c in range(3):
+        m_s[c].wait_recv()
+        m_f[c].wait_recv()
+        c_h.append(send(mbuf.at[c, 3, pl.ds(48, 16)], halo.at[0, c], NXT))
+        c_h.append(send(mbuf.at[c, 0, pl.ds(0, 16)], halo.at[1, c], PRV))
+        full = mbuf[c].reshape(256, 512)
+        for t in range(5):
+            taps[t] = taps[t] + nn_dot(full, up[t, c * 512 : (c + 1) * 512, :])
+
+    def edge(side, t):
+        return sum(nn_dot(halo[side, c], up[t, c * 512 : (c + 1) * 512, :]) for c in range(3))
+
     for c in c_h:
         c.wait_recv()
     has_prev = (s > 0).astype(F32)
     has_next = (s < 63).astype(F32)
-    lo = [nn_dot(halo[0], up[t]) * has_prev for t in (0, 1)]
-    hi = [nn_dot(halo[1], up[t]) * has_next for t in (3, 4)]
+    lo = [edge(0, t) * has_prev for t in (0, 1)]
+    hi = [edge(1, t) * has_next for t in (3, 4)]
 
     def shifted(v, before, after, which):
         tbuf[which, 0:16, :] = before
@@ -425,11 +451,11 @@
             v((512, 384), BF16), v((1536,), F32), v((1536, 256), BF16), v((1536, 128), BF16),
             v((192, 1536), BF16), v((4, 384, 1536), BF16), v((5, 1536, 384), BF16), v((544, 384), BF16),
             v((3, 512, 128), F32), v((3, 544, 128), F32), v((4, 256, 384), BF16), v((4, 64, 384), BF16),
-            v((256, 1536), BF16), v((4, 8, 64, 128), BF16), v((64 * RA, 384), BF16),
-            v((64 * RB, 384), BF16), v((4, 512, 256), F32),
+            v((256, 1536), BF16), v((4, 8, 64, 128), BF16), v((2, 64, 384), BF16), v((32, 5 * RA, 128), BF16),
+            v((32, 5 * RB, 128), BF16), v((4, 512, 256), F32),
             v((2, 256, 384), F32), v((3, 256, 384), BF16), v((3, 256, 384), BF16),
             v((3, 512, 256), BF16), v((3, 512, 256), BF16),
-            v((4, 64, 1536), BF16), v((2, 16, 1536), BF16), v((4, 288, 384), F32), v((3, 512, 128), F32),
+            v((3, 4, 64, 512), BF16), v((2, 3, 16, 512), BF16), v((4, 288, 384), F32), v((3, 512, 128), F32),
             pltpu.SemaphoreType.DMA((8,)),
             pltpu.SemaphoreType.DMA((N_SEM,)),
             pltpu.SemaphoreType.DMA((N_SEM,)),

time: 82.5 us -> 81.1 us (0.983)
  Pallas kernels: 78.3 us -> 76.9 us
    pallas_call x1, Pallas kernels: 78.3 us -> 76.9 us  [per_device(): pl.pallas_call(kernel, out_shape=(jax.ShapeDtypeStruct((512, 384), BF16),...]
where the time goes in v3:
time: 81.1 us; the launch traced here: 81 us
  Pallas kernels  76.9 us (95%)
  local copies, waits for them, and re-layouts  3.4 us (4%)
    pallas_call x1, Pallas kernels, per_device(): pl.pallas_call(kernel, out_shape=(jax.ShapeDtypeStruct((512, 384), BF16),...  76.9 us
    unnamed x2, local copies, waits for them, and re-layouts  3.4 us

profile of v3, /device:TPU:1, one launch (start us, length us, event | category | flops | bytes accessed | tf_op | source)
XLA Modules:
  0.0 81.0 jit_solution(17276165793473503766)
XLA Ops:
  0.6 76.9 %shard_map.95 = (bf16[512,384]{1,0:T(8,128)(2,1)}, bf16[256,384]{1,0:T(8,128)(2,1)}) custom-call(bf16[512,384]{1,0:T(8,128)(2,1)} %level_hbm.1, f32[1536]{0:T(1024)} %gain_hbm.1, bf16[1536,256]{1,0:T(8,128)(2,1)} %wq_hbm.1, bf16[1536,128]{1,0:T(8,128)(2,1)} %wk_hbm.1, bf16[192,1536]{1,0:T(8,128)(2,1)} %bitcast.1, bf16[384,1536]{1,0:T(8,128)(2,1)} %wo_hbm.1, ...), custom_call_target="tpu_custom_call" | custom-call | tf_op jit(solution)/shard_map/pallas_call | solution.py:442
  77.6 1.8 %copy.12 = bf16[512,384]{1,0:T(8,128)(2,1)} copy(bf16[512,384]{1,0:T(8,128)(2,1)} %get-tuple-element.4) | data formatting | bytes 786432
  79.3 1.6 %copy.13 = bf16[256,384]{1,0:T(8,128)(2,1)} copy(bf16[256,384]{1,0:T(8,128)(2,1)} %get-tuple-element.5) | data formatting | bytes 393216

commit v4 on v3

--- a/solution.py
+++ b/solution.py
@@ -467,7 +467,16 @@
         level_input, norm_gain, query_weight, key_weight, value_weight.T,
         out_weight, up_weight, grad_output,
     )
-    return outs
+    def emit(a, b, c, d):
+        c[...] = a[...]
+        d[...] = b[...]
+
+    return pl.pallas_call(
+        emit,
+        out_shape=tuple(jax.ShapeDtypeStruct(o.shape, o.dtype) for o in outs),
+        in_specs=[vmem] * 2,
+        out_specs=(vmem, vmem),
+    )(*outs)
 
 
 def solution(mesh):

time: 81.1 us -> 79.5 us (0.980)
  local copies, waits for them, and re-layouts: 3.4 us -> 0 us
  Pallas kernels: 76.9 us -> 78.8 us
    unnamed x2 -> x0, local copies, waits for them, and re-layouts: 3.4 us -> none
    pallas_call x0 -> x1, Pallas kernels: none -> 1.89 us  [per_device(): pl.pallas_call(emit, out_shape=tuple((jax.ShapeDtypeStruct(o.shape, o.dty...]
where the time goes in v4:
time: 79.5 us; the launch traced here: 79.4 us
  Pallas kernels  78.8 us (99%)
    pallas_call x1, Pallas kernels, per_device(): pl.pallas_call(kernel, out_shape=(jax.ShapeDtypeStruct((512, 384), BF16),...  76.9 us
    pallas_call x1, Pallas kernels, per_device(): pl.pallas_call(emit, out_shape=tuple((jax.ShapeDtypeStruct(o.shape, o.dty...  1.89 us

profile of v4, /device:TPU:1, one launch (start us, length us, event | category | flops | bytes accessed | tf_op | source)
XLA Modules:
  0.0 79.4 jit_solution(7063852425975827467)
XLA Ops:
  0.6 76.9 %shard_map.95 = (bf16[512,384]{1,0:T(8,128)(2,1)}, bf16[256,384]{1,0:T(8,128)(2,1)}) custom-call(bf16[512,384]{1,0:T(8,128)(2,1)} %level_hbm.1, f32[1536]{0:T(1024)} %gain_hbm.1, bf16[1536,256]{1,0:T(8,128)(2,1)} %wq_hbm.1, bf16[1536,128]{1,0:T(8,128)(2,1)} %wk_hbm.1, bf16[192,1536]{1,0:T(8,128)(2,1)} %bitcast.1, bf16[384,1536]{1,0:T(8,128)(2,1)} %wo_hbm.1, ...), custom_call_target="tpu_custom_call" | custom-call | tf_op jit(solution)/shard_map/pallas_call | solution.py:442
  77.6 1.9 %shard_map.96 = (bf16[512,384]{1,0:T(8,128)(2,1)}, bf16[256,384]{1,0:T(8,128)(2,1)}) custom-call(bf16[512,384]{1,0:T(8,128)(2,1)} %get-tuple-element.4.a, bf16[256,384]{1,0:T(8,128)(2,1)} %get-tuple-element.5.b), custom_call_target="tpu_custom_call" | custom-call | tf_op jit(solution)/shard_map/pallas_call | solution.py:474
